TPU v7x, 32 devices: a whole 2x2x4 slice. The times are simulated.
32 devices in a mesh: img: 8 (over z, y), shot: 4 (over x, core).
Axes of the slice: x: 2, y: 2, z: 4, core: 2. Of those that a mesh axis runs over, the one named last changes fastest.
Arguments:
- shot_green: bfloat16 [2, 3584, 1024], P(None, 'img', 'shot'), may hold values from -6 to 6
- rec_green: bfloat16 [2, 3584, 3584], P(None, 'img'), may hold values from -0.0625 to 0.0625
- model: float32 [3584], P('img'), may hold values from 0.2 to 2
- hadamard_order: int32 [256], replicated, may hold values from 0 to 255, each once
- shot_signs: int32 [1024], P('shot'), may hold values from 0 to 1
Outputs:
- born_data: bfloat16 [2, 3584, 1024], P(None, 'img', 'shot')
Inputs may be any that keep to these rules, and one draw needn't show every extreme that they name: `hadamard_order`: each of 0 to 255 once.
All inputs are finite; a program needn't handle non-finite values.
Results may differ from a plain program's by a relative error of at most 0.0049.
Values may be sent and summed in bfloat16 or wider, within the bound.
A program may use at most 128 MiB of HBM per device.

v0:
```python
import jax
import jax.numpy as jnp
from jax import lax
from jax.sharding import PartitionSpec as P


def parity(values, bit_count):
    result = jnp.zeros_like(values)
    for shift_by in range(bit_count):
        result = jnp.bitwise_xor(result, jnp.bitwise_and(jnp.right_shift(values, shift_by), 1))
    return result


def on_device(shot_green, rec_green, model, hadamard_order, shot_signs):
    shot_local = shot_green.shape[2]
    x_local = shot_green.shape[1]
    blocks = lax.axis_size("shot")
    block_bits = blocks.bit_length() - 1
    columns = jnp.arange(shot_local, dtype=jnp.int32)
    local_code = (
        1
        - 2
        * parity(
            jnp.bitwise_and(hadamard_order[:, None], columns[None, :]), shot_local.bit_length() - 1
        )
    ).astype(jnp.float32)
    signs = (1 - 2 * shot_signs).astype(jnp.float32)
    signed_field = shot_green.astype(jnp.float32) * signs[None, None, :]
    coded = jnp.einsum("pxd,bd->pxb", signed_field, local_code, precision=lax.Precision.HIGHEST)
    my_index = lax.axis_index("shot")
    gathered = lax.all_gather(coded, "shot", axis=2, tiled=True).reshape(
        2, x_local, blocks, shot_local
    )
    block_ids = jnp.arange(blocks, dtype=jnp.int32)
    weights = (1 - 2 * parity(jnp.bitwise_and(my_index, block_ids), block_bits)).astype(jnp.float32)
    encoded = jnp.einsum("pxcb,c->pxb", gathered, weights, precision=lax.Precision.HIGHEST)
    scaled = (model[None, :, None] * encoded * (blocks * shot_local) ** (-0.5)).astype(jnp.bfloat16)
    block_rows = lax.all_gather(scaled, "img", axis=1, tiled=True)
    real_part = jnp.dot(rec_green[0], block_rows[0], preferred_element_type=jnp.float32) - jnp.dot(
        rec_green[1], block_rows[1], preferred_element_type=jnp.float32
    )
    imag_part = jnp.dot(rec_green[0], block_rows[1], preferred_element_type=jnp.float32) + jnp.dot(
        rec_green[1], block_rows[0], preferred_element_type=jnp.float32
    )
    summed = jnp.stack((real_part, imag_part))
    return summed.astype(jnp.bfloat16)


def solution(mesh):
    placed = (P(None, "img", "shot"), P(None, "img", None), P("img"), P(), P("shot"))
    return jax.shard_map(
        on_device, mesh=mesh, in_specs=placed, out_specs=P(None, "img", "shot"), check_vma=False
    )
```

profile of v0, /device:TPU:0, one launch (start us, length us, event | category | flops | bytes accessed | tf_op | source)
XLA Modules:
  0.0 142.5 jit_solution(3556827245080371166)
XLA Ops:
  6.5 0.0 all-gather.3.cloned.1.call-start
  6.5 0.7 subtract_convert_fusion
  7.2 3.1 %fusion.32 = f32[2,448,256]{2,1,0:T(8,128)} fusion(bf16[2,448,256]{2,1,0:T(8,128)(2,1)} %param.5, f32[256]{0:T(256)S(1)} %subtract_convert_fusion, s32[256]{0:T(256)} %param.8), kind=kOutput, calls=%fused_computation.23 | convolution fusion | flops 706871296 | bytes 1378304 | tf_op jit(solution)/shard_map/pxd,bd->pxb/dot_general | solution.py:29
  10.4 0.0 all-gather.3.cloned.1.call-update
  10.4 0.0 all-gather.5.cloned.1.call-start
  10.4 34.3 %all-gather.3.cloned.1.call-done = f32[2,448,1024]{2,1,0:T(8,128)} async-done(((f32[2,448,256]{2,1,0:T(8,128)}), f32[2,448,1024]{2,1,0:T(8,128)}) %all-gather.3.cloned.1.call-update) | async-done | bytes 3670032 | tf_op jit(solution)/shard_map/all_gather | solution.py:31
  44.7 5.3 %reshape.6 = f32[2,448,4,256]{3,2,1,0:T(4,128)} reshape(f32[2,448,1024]{2,1,0:T(8,128)} %all-gather.3.cloned.1.call-done) | data formatting | bytes 7340032 | tf_op jit(solution)/shard_map/reshape | solution.py:31
  50.1 0.0 copy-start
  50.1 8.1 %fusion.74 = f32[1,2,448,256]{3,0,2,1:T(1,128)S(1)} fusion(f32[2,448,4,256]{3,2,1,0:T(4,128)} %reshape.6, s32[]{:T(128)S(6)} %axis_index.12), kind=kOutput, calls=%fused_computation.67 | convolution fusion | flops 11010084 | bytes 4587524 | tf_op jit(solution)/shard_map/pxcb,c->pxb/dot_general | solution.py:36
  58.2 0.0 copy-done
  58.2 0.9 fusion.31
  59.1 0.0 all-gather.5.cloned.1.call-update
  59.1 67.0 %all-gather.5.cloned.1.call-done = bf16[2,3584,256]{2,1,0:T(8,128)(2,1)} async-done(((bf16[2,448,256]{2,1,0:T(8,128)(2,1)}), bf16[2,3584,256]{2,1,0:T(8,128)(2,1)}) %all-gather.5.cloned.1.call-update) | async-done | bytes 3670032 | tf_op jit(solution)/shard_map/all_gather | solution.py:38
  126.1 0.0 copy-start.1
  126.1 0.0 slice-start
  126.1 3.6 %fusion = f32[256,448]{0,1:T(8,128)S(1)} fusion(bf16[2,448,3584]{2,1,0:T(8,128)(2,1)} %param.6, bf16[2,3584,256]{2,1,0:T(8,128)(2,1)} %all-gather.5.cloned.1.call-done), kind=kOutput, calls=%fused_computation | convolution fusion | flops 822083584 | bytes 5505024 | tf_op jit(solution)/shard_map/dot_general | solution.py:39
  129.7 0.0 copy-done.1
  129.7 0.0 slice-start.1
  129.7 3.1 %fusion.2 = f32[256,448]{0,1:T(8,128)S(1)} fusion(bf16[2,448,3584]{2,1,0:T(8,128)(2,1)} %param.6, bf16[2,3584,256]{2,1,0:T(8,128)(2,1)S(1)} %copy-done.1), kind=kOutput, calls=%fused_computation.2 | convolution fusion | flops 822083584 | bytes 5505024 | tf_op jit(solution)/shard_map/dot_general | solution.py:42
  132.8 0.0 slice-done
  132.8 0.0 slice-done.1
  132.9 1.0 fusion.27
  133.9 1.0 fusion.24
  134.9 0.8 pad_maximum_fusion
  (1 shorter events, 0.0 us)
Async XLA Ops:
  6.5 38.2 %all-gather.3.cloned.1.call-start = ((), (), s32[]{:S(2)}) async-start(), calls=%async_computation | async-start | bytes 4587520 | tf_op jit(solution)/shard_map/all_gather | solution.py:31
  10.4 115.7 %all-gather.5.cloned.1.call-start = ((), (), s32[]{:S(2)}) async-start(), calls=%async_computation.1 | async-start | bytes 4128768 | tf_op jit(solution)/shard_map/all_gather | solution.py:38
  50.1 8.1 %copy-start = (f32[448]{0:T(512)S(1)}, f32[448]{0:T(512)}, u32[]{:S(2)}) copy-start(f32[448]{0:T(512)} %param.7) | copy-start | bytes 5380
  126.1 3.6 %copy-start.1 = (bf16[2,3584,256]{2,1,0:T(8,128)(2,1)S(1)}, bf16[2,3584,256]{2,1,0:T(8,128)(2,1)}, u32[]{:S(2)}) copy-start(bf16[2,3584,256]{2,1,0:T(8,128)(2,1)} %all-gather.5.cloned.1.call-done) | copy-start | bytes 11010052
  126.1 6.7 %slice-start = ((s8[6422528]{0:T(1024)(128)(4,1)}), s8[4194304]{0:T(1024)(128)(4,1)S(1)}, s32[]{:S(2)}) async-start(s8[6422528]{0:T(1024)(128)(4,1)} %bitcast.65), calls=%async_computation.2 | async-start | bytes 8388608
  129.7 3.1 %slice-start.1 = ((s8[6422528]{0:T(1024)(128)(4,1)}), s8[2228224]{0:T(1024)(128)(4,1)S(1)}, s32[]{:S(2)}) async-start(s8[6422528]{0:T(1024)(128)(4,1)} %bitcast.65), calls=%async_computation.3 | async-start | bytes 4456448
Sparse Core Ops, SparseCore 0:
  10.5 34.1 all-gather.2
  59.2 66.8 all-gather.4
where the time goes:
time: 143 us
  waiting for transfers between devices  101 us (71%)
  matrix products  19.9 us (14%)
  between operations  13.5 us (9%)
  local copies, waits for them, and re-layouts  5.37 us (4%)
  other arithmetic  2.41 us (2%)
    all_gather x1, waiting for transfers between devices, on_device(): block_rows = lax.all_gather(scaled, 'img', axis=1, tiled=True)  67 us
    all_gather x1, waiting for transfers between devices, on_device(): lax.all_gather(coded, 'shot', axis=2, tiled=True)  34.3 us
    dot_general x1, matrix products, on_device(): jnp.einsum('pxcb,c->pxb', gathered, weights, precision=lax.Precision.HIGH...  8.07 us
    reshape x1, local copies, waits for them, and re-layouts, on_device(): lax.all_gather(coded, 'shot', axis=2, tiled=True)  5.35 us
    dot_general x1, matrix products, on_device(): jnp.dot(rec_green[1], block_rows[1], preferred_element_type=jnp.float32)  3.6 us
    dot_general x1, matrix products, on_device(): jnp.einsum('pxd,bd->pxb', signed_field, local_code, precision=lax.Precisi...  3.14 us
    dot_general x1, matrix products, on_device(): jnp.dot(rec_green[1], block_rows[0], preferred_element_type=jnp.float32)  3.08 us
  transfers between devices with their start and end apart: 2, of which 2 were waited for; matrix products, arithmetic and copies ran while one was open for 0% of the time, Pallas kernels for 0%

commit v1 on v0

--- a/solution.py
+++ b/solution.py
@@ -35,7 +35,12 @@
     weights = (1 - 2 * parity(jnp.bitwise_and(my_index, block_ids), block_bits)).astype(jnp.float32)
     encoded = jnp.einsum("pxcb,c->pxb", gathered, weights, precision=lax.Precision.HIGHEST)
     scaled = (model[None, :, None] * encoded * (blocks * shot_local) ** (-0.5)).astype(jnp.bfloat16)
-    block_rows = lax.all_gather(scaled, "img", axis=1, tiled=True)
+    ring = [scaled]
+    for hop in range(7):
+        ring.append(lax.ppermute(ring[-1], "img", [(dev, (dev + 1) % 8) for dev in range(8)]))
+    block_rows = jnp.roll(
+        jnp.concatenate(ring[::-1], axis=1), (lax.axis_index("img") + 1) * ring[0].shape[1], axis=1
+    )
     real_part = jnp.dot(rec_green[0], block_rows[0], preferred_element_type=jnp.float32) - jnp.dot(
         rec_green[1], block_rows[1], preferred_element_type=jnp.float32
     )

time: 143 us -> 167 us (1.17)
  waiting for transfers between devices: 101 us -> 124 us
  local copies, waits for them, and re-layouts: 5.37 us -> 10.2 us
  matrix products: 19.9 us -> 15.3 us
    ppermute x0 -> x7, waiting for transfers between devices: none -> 89.3 us  [on_device(): lax.ppermute(ring[-1], 'img', [(dev, (dev + 1) % 8) for dev in range(8)])]
    all_gather x1 -> x0, waiting for transfers between devices: 67 us -> none  [on_device(): block_rows = lax.all_gather(scaled, 'img', axis=1, tiled=True)]
    unnamed x8 -> x20, local copies, waits for them, and re-layouts: 0.02 us -> 4.84 us
    dot_general x1, matrix products: 3.6 us -> 1.04 us  [on_device(): jnp.dot(rec_green[1], block_rows[1], preferred_element_type=jnp.float32)]
    dot_general x1, matrix products: 3.08 us -> 1.04 us  [on_device(): jnp.dot(rec_green[1], block_rows[0], preferred_element_type=jnp.float32)]
  transfers between devices with their start and end apart: 2 -> 8, of which waited for: 2 -> 8; matrix products, arithmetic and copies ran while one was open for 0% -> 0% of each run, Pallas kernels for 0% -> 0%
where the time goes in v1:
time: 167 us; the launch traced here: 166 us
  waiting for transfers between devices  124 us (74%)
  matrix products  15.3 us (9%)
  between operations  13.6 us (8%)
  local copies, waits for them, and re-layouts  10.2 us (6%)
  other arithmetic  1.92 us (1%)
    ppermute x7, waiting for transfers between devices, on_device(): lax.ppermute(ring[-1], 'img', [(dev, (dev + 1) % 8) for dev in range(8)])  89.3 us
    all_gather x1, waiting for transfers between devices, on_device(): lax.all_gather(coded, 'shot', axis=2, tiled=True)  34.4 us
    dot_general x1, matrix products, on_device(): jnp.einsum('pxcb,c->pxb', gathered, weights, precision=lax.Precision.HIGH...  8.05 us
    reshape x1, local copies, waits for them, and re-layouts, on_device(): lax.all_gather(coded, 'shot', axis=2, tiled=True)  5.36 us
    unnamed x20, local copies, waits for them, and re-layouts  4.84 us
  transfers between devices with their start and end apart: 8, of which 8 were waited for; matrix products, arithmetic and copies ran while one was open for 0% of the time, Pallas kernels for 0%

profile of v1, /device:TPU:0, one launch (start us, length us, event | category | flops | bytes accessed | tf_op | source)
XLA Modules:
  0.0 166.3 jit_solution(5423135321806397520)
XLA Ops:
  6.5 0.7 subtract_convert_fusion
  7.2 3.1 %fusion.32 = f32[2,448,256]{2,1,0:T(8,128)} fusion(bf16[2,448,256]{2,1,0:T(8,128)(2,1)} %param.5, f32[256]{0:T(256)S(1)} %subtract_convert_fusion, s32[256]{0:T(256)} %param.8), kind=kOutput, calls=%fused_computation.23 | convolution fusion | flops 706871296 | bytes 1378304 | tf_op jit(solution)/shard_map/pxd,bd->pxb/dot_general | solution.py:29
  10.4 34.4 %all-gather.2.cloned.1.call-done = f32[2,448,1024]{2,1,0:T(8,128)} async-done(((f32[2,448,256]{2,1,0:T(8,128)}), f32[2,448,1024]{2,1,0:T(8,128)}) %all-gather.2.cloned.1.call-update) | async-done | bytes 3670032 | tf_op jit(solution)/shard_map/all_gather | solution.py:31
  44.8 5.4 %reshape.6 = f32[2,448,4,256]{3,2,1,0:T(4,128)} reshape(f32[2,448,1024]{2,1,0:T(8,128)} %all-gather.2.cloned.1.call-done) | data formatting | bytes 7340032 | tf_op jit(solution)/shard_map/reshape | solution.py:31
  50.1 8.1 %fusion.74 = f32[1,2,448,256]{3,0,2,1:T(1,128)S(1)} fusion(f32[2,448,4,256]{3,2,1,0:T(4,128)} %reshape.6, s32[]{:T(128)S(6)} %axis_index.22), kind=kOutput, calls=%fused_computation.83 | convolution fusion | flops 11010084 | bytes 4587524 | tf_op jit(solution)/shard_map/pxcb,c->pxb/dot_general | solution.py:36
  58.2 0.1 fusion.31
  58.3 1.5 collective-permute-start
  59.9 13.9 %collective-permute-done = bf16[2,448,256]{2,1,0:T(8,128)(2,1)S(1)} collective-permute-done((bf16[2,448,256]{2,1,0:T(8,128)(2,1)S(1)}, bf16[2,448,256]{2,1,0:T(8,128)(2,1)S(1)}, u32[]{:S(2)}, u32[]{:S(2)}) %collective-permute-start) | collective-permute-done | bytes 458784 | tf_op jit(solution)/shard_map/ppermute | solution.py:40
  73.8 14.5 %collective-permute-done.1 = bf16[2,448,256]{2,1,0:T(8,128)(2,1)S(1)} collective-permute-done((bf16[2,448,256]{2,1,0:T(8,128)(2,1)S(1)}, bf16[2,448,256]{2,1,0:T(8,128)(2,1)S(1)}, u32[]{:S(2)}, u32[]{:S(2)}) %collective-permute-start.1) | collective-permute-done | bytes 458784 | tf_op jit(solution)/shard_map/ppermute | solution.py:40
  88.3 13.6 %collective-permute-done.2 = bf16[2,448,256]{2,1,0:T(8,128)(2,1)S(1)} collective-permute-done((bf16[2,448,256]{2,1,0:T(8,128)(2,1)S(1)}, bf16[2,448,256]{2,1,0:T(8,128)(2,1)S(1)}, u32[]{:S(2)}, u32[]{:S(2)}) %collective-permute-start.2) | collective-permute-done | bytes 458784 | tf_op jit(solution)/shard_map/ppermute | solution.py:40
  101.9 12.7 %collective-permute-done.3 = bf16[2,448,256]{2,1,0:T(8,128)(2,1)S(1)} collective-permute-done((bf16[2,448,256]{2,1,0:T(8,128)(2,1)S(1)}, bf16[2,448,256]{2,1,0:T(8,128)(2,1)S(1)}, u32[]{:S(2)}, u32[]{:S(2)}) %collective-permute-start.3) | collective-permute-done | bytes 458784 | tf_op jit(solution)/shard_map/ppermute | solution.py:40
  114.6 11.8 %collective-permute-done.4 = bf16[2,448,256]{2,1,0:T(8,128)(2,1)S(1)} collective-permute-done((bf16[2,448,256]{2,1,0:T(8,128)(2,1)S(1)}, bf16[2,448,256]{2,1,0:T(8,128)(2,1)S(1)}, u32[]{:S(2)}, u32[]{:S(2)}) %collective-permute-start.4) | collective-permute-done | bytes 458784 | tf_op jit(solution)/shard_map/ppermute | solution.py:40
  126.4 11.3 %collective-permute-done.5 = bf16[2,448,256]{2,1,0:T(8,128)(2,1)} collective-permute-done((bf16[2,448,256]{2,1,0:T(8,128)(2,1)S(1)}, bf16[2,448,256]{2,1,0:T(8,128)(2,1)}, u32[]{:S(2)}, u32[]{:S(2)}) %collective-permute-start.5) | collective-permute-done | bytes 458784 | tf_op jit(solution)/shard_map/ppermute | solution.py:40
  137.7 11.5 %collective-permute-done.6 = bf16[2,448,256]{2,1,0:T(8,128)(2,1)} collective-permute-done((bf16[2,448,256]{2,1,0:T(8,128)(2,1)}, bf16[2,448,256]{2,1,0:T(8,128)(2,1)}, u32[]{:S(2)}, u32[]{:S(2)}) %collective-permute-start.6) | collective-permute-done | bytes 458784 | tf_op jit(solution)/shard_map/ppermute | solution.py:40
  149.2 1.0 constant_dynamic-update-slice_fusion.15
  150.2 1.2 constant_dynamic-update-slice_fusion.14
  151.6 0.1 constant_dynamic-update-slice_fusion.8
  151.8 1.2 constant_dynamic-update-slice_fusion.7
  153.0 1.1 constant_dynamic-update-slice_fusion.6
  154.4 1.0 fusion.2
  155.5 1.0 fusion
  156.5 1.0 fusion.27
  157.6 1.0 fusion.24
  158.6 0.8 pad_maximum_fusion
  (26 shorter events, 0.5 us)
Async XLA Ops:
  6.5 38.2 %all-gather.2.cloned.1.call-start = ((), (), s32[]{:S(2)}) async-start(), calls=%async_computation | async-start | bytes 4587520 | tf_op jit(solution)/shard_map/all_gather | solution.py:31
  7.2 51.0 %copy-start = (f32[448]{0:T(512)S(1)}, f32[448]{0:T(512)}, u32[]{:S(2)}) copy-start(f32[448]{0:T(512)} %param.7) | copy-start | bytes 5380
  58.3 15.4 %collective-permute-start = (bf16[2,448,256]{2,1,0:T(8,128)(2,1)S(1)}, bf16[2,448,256]{2,1,0:T(8,128)(2,1)S(1)}, u32[]{:S(2)}, u32[]{:S(2)}) collective-permute-start(bf16[2,448,256]{2,1,0:T(8,128)(2,1)S(1)} %fusion.31), channel_id=1, source_target_pairs={{0,4},{4,8},{8,12},{12,16},{16,20},{20,24},{24,28},{28,0},{1,5},{5... | collective-permute-start | bytes 1376264 | tf_op jit(solution)/shard_map/ppermute | solution.py:40
  73.8 14.5 %collective-permute-start.1 = (bf16[2,448,256]{2,1,0:T(8,128)(2,1)S(1)}, bf16[2,448,256]{2,1,0:T(8,128)(2,1)S(1)}, u32[]{:S(2)}, u32[]{:S(2)}) collective-permute-start(bf16[2,448,256]{2,1,0:T(8,128)(2,1)S(1)} %collective-permute-done), channel_id=1, source_target_pairs={{0,4},{4,8},{8,12},{12,16},{16,20},{20,24},{24,28},{28,0},{1,5},{5... | collective-permute-start | bytes 1376264 | tf_op jit(solution)/shard_map/ppermute | solution.py:40
  88.3 13.6 %collective-permute-start.2 = (bf16[2,448,256]{2,1,0:T(8,128)(2,1)S(1)}, bf16[2,448,256]{2,1,0:T(8,128)(2,1)S(1)}, u32[]{:S(2)}, u32[]{:S(2)}) collective-permute-start(bf16[2,448,256]{2,1,0:T(8,128)(2,1)S(1)} %collective-permute-done.1), channel_id=1, source_target_pairs={{0,4},{4,8},{8,12},{12,16},{16,20},{20,24},{24,28},{28,0},{1,5},{5... | collective-permute-start | bytes 1376264 | tf_op jit(solution)/shard_map/ppermute | solution.py:40
  101.9 12.7 %collective-permute-start.3 = (bf16[2,448,256]{2,1,0:T(8,128)(2,1)S(1)}, bf16[2,448,256]{2,1,0:T(8,128)(2,1)S(1)}, u32[]{:S(2)}, u32[]{:S(2)}) collective-permute-start(bf16[2,448,256]{2,1,0:T(8,128)(2,1)S(1)} %collective-permute-done.2), channel_id=1, source_target_pairs={{0,4},{4,8},{8,12},{12,16},{16,20},{20,24},{24,28},{28,0},{1,5},{5... | collective-permute-start | bytes 1376264 | tf_op jit(solution)/shard_map/ppermute | solution.py:40
  114.6 11.8 %collective-permute-start.4 = (bf16[2,448,256]{2,1,0:T(8,128)(2,1)S(1)}, bf16[2,448,256]{2,1,0:T(8,128)(2,1)S(1)}, u32[]{:S(2)}, u32[]{:S(2)}) collective-permute-start(bf16[2,448,256]{2,1,0:T(8,128)(2,1)S(1)} %collective-permute-done.3), channel_id=1, source_target_pairs={{0,4},{4,8},{8,12},{12,16},{16,20},{20,24},{24,28},{28,0},{1,5},{5... | collective-permute-start | bytes 1376264 | tf_op jit(solution)/shard_map/ppermute | solution.py:40
  126.4 11.3 %collective-permute-start.5 = (bf16[2,448,256]{2,1,0:T(8,128)(2,1)S(1)}, bf16[2,448,256]{2,1,0:T(8,128)(2,1)}, u32[]{:S(2)}, u32[]{:S(2)}) collective-permute-start(bf16[2,448,256]{2,1,0:T(8,128)(2,1)S(1)} %collective-permute-done.4), channel_id=1, source_target_pairs={{0,4},{4,8},{8,12},{12,16},{16,20},{20,24},{24,28},{28,0},{1,5},{5... | collective-permute-start | bytes 1376264 | tf_op jit(solution)/shard_map/ppermute | solution.py:40
  137.7 11.5 %collective-permute-start.6 = (bf16[2,448,256]{2,1,0:T(8,128)(2,1)}, bf16[2,448,256]{2,1,0:T(8,128)(2,1)}, u32[]{:S(2)}, u32[]{:S(2)}) collective-permute-start(bf16[2,448,256]{2,1,0:T(8,128)(2,1)} %collective-permute-done.5), channel_id=1, source_target_pairs={{0,4},{4,8},{8,12},{12,16},{16,20},{20,24},{24,28},{28,0},{1,5},{5... | collective-permute-start | bytes 1376264 | tf_op jit(solution)/shard_map/ppermute | solution.py:40
  150.2 4.2 %slice-start = ((s8[6422528]{0:T(1024)(128)(4,1)}), s8[4194304]{0:T(1024)(128)(4,1)S(1)}, s32[]{:S(2)}) async-start(s8[6422528]{0:T(1024)(128)(4,1)} %bitcast.69), calls=%async_computation.1 | async-start | bytes 8388608
  151.8 2.6 %slice-start.1 = ((s8[6422528]{0:T(1024)(128)(4,1)}), s8[2228224]{0:T(1024)(128)(4,1)S(1)}, s32[]{:S(2)}) async-start(s8[6422528]{0:T(1024)(128)(4,1)} %bitcast.69), calls=%async_computation.2 | async-start | bytes 4456448
Sparse Core Ops, SparseCore 0:
  10.5 34.1 all-gather.1
